TPU v7x, 32 devices: a whole 2x2x4 slice. The times are simulated.
32 devices in a mesh: outer: 4 (over y, x), inner: 8 (over z, core).
Axes of the slice: x: 2, y: 2, z: 4, core: 2. Of those that a mesh axis runs over, the one named last changes fastest.
Arguments:
- queries: bfloat16 [8192, 2048], P(('outer', 'inner')), may hold values from -4 to 4
- key_rows: bfloat16 [8192, 128], P(('outer', 'inner')), may hold values from -4 to 4
- value_rows: bfloat16 [8192, 128], P(('outer', 'inner')), may hold values from -6 to 6
- out_grad: bfloat16 [8192, 2048], P(('outer', 'inner')), may hold values from -96 to 96
- outputs: bfloat16 [8192, 2048], P(('outer', 'inner')), may hold values from -1.75 to 1.75
- log_sum: float32 [16, 8192], P(None, ('outer', 'inner')), may hold values from 6 to 7.5
- span_table: int32 [32, 2], replicated, may hold values from 0 to 63, as said below
Outputs:
- query_grad: bfloat16 [8192, 2048], P(('outer', 'inner'))
- key_grad: float32 [8192, 128], P(('outer', 'inner'))
- value_grad: float32 [8192, 128], P(('outer', 'inner'))
Inputs may be any that keep to these rules, and one draw needn't show every extreme that they name: `span_table`: row e holds spans p and 63 - p, where p over the rows is a permutation of 0 to 31.
All inputs are finite; a program needn't handle non-finite values.
Results may differ from a plain program's by a relative error of at most 0.0075.
Values may be sent and summed in bfloat16 or wider, within the bound.
A program may use at most 64 MiB of HBM per device.

v0:
```python
import math

import jax
import jax.numpy as jnp
from jax import lax
from jax.sharding import PartitionSpec as P

OUT_STEPS = 2
IN_STEPS = 2


def shifted(shard, axis, by):
    devices = lax.axis_size(axis)
    return lax.ppermute(shard, axis, [(i, (i + by) % devices) for i in range(devices)])


def block_grads(
    query_block, key_block, value_block, grad_block, log_block, row_dot, query_pos, key_pos, factor
):
    scores = (
        jnp.einsum("qgd,kd->gqk", query_block, key_block, preferred_element_type=jnp.float32)
        * factor
    )
    visible = key_pos[None, None, :] <= query_pos[None, :, None]
    weights = jnp.where(visible, jnp.exp(scores - log_block[:, :, None]), 0.0)
    dweights = jnp.einsum(
        "qgd,kd->gqk", grad_block, value_block, preferred_element_type=jnp.float32
    )
    dscores = weights * (dweights - row_dot[:, :, None])
    weights_low = weights.astype(jnp.bfloat16)
    dscores_low = dscores.astype(jnp.bfloat16)
    value_part = jnp.einsum(
        "gqk,qgd->kd", weights_low, grad_block, preferred_element_type=jnp.float32
    )
    key_part = jnp.einsum(
        "gqk,qgd->kd", dscores_low, query_block, preferred_element_type=jnp.float32
    )
    query_part = jnp.einsum(
        "gqk,kd->qgd", dscores_low, key_block, preferred_element_type=jnp.float32
    )
    return (query_part, key_part, value_part)


def per_device(queries, key_rows, value_rows, out_grad, outputs, log_sum, span_table):
    head_count = log_sum.shape[0]
    head_size = key_rows.shape[1]
    row_count = key_rows.shape[0]
    span_rows = row_count // 2
    factor = 1.0 / math.sqrt(head_size)
    query_block = queries.reshape(row_count, head_count, head_size)
    grad_block = out_grad.reshape(row_count, head_count, head_size)
    row_dot = jnp.sum(
        grad_block.astype(jnp.float32)
        * outputs.reshape(row_count, head_count, head_size).astype(jnp.float32),
        axis=-1,
    ).T
    outer_count = lax.axis_size("outer")
    inner_count = lax.axis_size("inner")
    outer_index = lax.axis_index("outer")
    inner_index = lax.axis_index("inner")
    offsets = jnp.arange(span_rows, dtype=jnp.int32)

    def block_spans(a, b):
        source = (outer_index - a) % outer_count * inner_count + (inner_index - b) % inner_count
        return span_table[source]

    def positions(spans):
        return (spans[:, None] * span_rows + offsets[None, :]).reshape(row_count)

    own_spans = block_spans(0, 0)
    query_pos = positions(own_spans)
    query_total = jnp.zeros((row_count, head_count, head_size), jnp.float32)
    zero_rows = jnp.zeros((row_count, head_size), jnp.float32)
    key_total = zero_rows
    value_total = zero_rows
    group_block = (key_rows, value_rows)
    for a in range(OUT_STEPS):
        if a > 0:
            group_block = shifted((group_block[0], group_block[1]), "outer", 1)
        travel = group_block
        carried = (zero_rows, zero_rows)
        for b in range(IN_STEPS):
            if b > 0:
                travel = shifted((travel[0], travel[1]), "inner", 1)
                carried = (
                    shifted(carried[0].astype(jnp.bfloat16), "inner", 1).astype(jnp.float32),
                    shifted(carried[1].astype(jnp.bfloat16), "inner", 1).astype(jnp.float32),
                )
            key_spans = block_spans(a, b)
            query_part, key_part, value_part = block_grads(
                query_block,
                travel[0],
                travel[1],
                grad_block,
                log_sum,
                row_dot,
                query_pos,
                positions(key_spans),
                factor,
            )
            query_total = query_total + query_part
            carried = (carried[0] + key_part, carried[1] + value_part)
        carried = shifted((carried[0], carried[1]), "inner", 1 - IN_STEPS)
        if a > 0:
            carried = shifted((carried[0], carried[1]), "outer", -a)
        key_total = key_total + carried[0]
        value_total = value_total + carried[1]
    query_grad = (
        (query_total * factor).reshape(row_count, head_count * head_size).astype(jnp.bfloat16)
    )
    return (query_grad, key_total * factor, value_total)


def solution(mesh):
    placed = (
        P(("outer", "inner"), None),
        P(("outer", "inner"), None),
        P(("outer", "inner"), None),
        P(("outer", "inner"), None),
        P(("outer", "inner"), None),
        P(None, ("outer", "inner")),
        P(),
    )
    return jax.shard_map(
        per_device,
        mesh=mesh,
        in_specs=placed,
        out_specs=(
            P(("outer", "inner"), None),
            P(("outer", "inner"), None),
            P(("outer", "inner"), None),
        ),
        check_vma=False,
    )
```

profile of v0, /device:TPU:0, one launch (start us, length us, event | category | flops | bytes accessed | tf_op | source)
XLA Modules:
  0.0 58.1 jit_solution(1103237823077157760)
XLA Ops:
  0.6 3.0 %collective-permute-start.3 = (bf16[256,128]{1,0:T(8,128)(2,1)}, bf16[256,128]{1,0:T(8,128)(2,1)S(1)}, u32[]{:S(2)}, u32[]{:S(2)}) collective-permute-start(bf16[256,128]{1,0:T(8,128)(2,1)} %param.9), channel_id=1, source_target_pairs={{0,8},{8,16},{16,24},{24,0},{1,9},{9,17},{17,25},{25,1},{2,10},{10... | collective-permute-start | bytes 196616 | tf_op jit(solution)/shard_map/ppermute | solution.py:14
  3.6 1.5 %collective-permute-start.2 = (bf16[256,128]{1,0:T(8,128)(2,1)}, bf16[256,128]{1,0:T(8,128)(2,1)S(1)}, u32[]{:S(2)}, u32[]{:S(2)}) collective-permute-start(bf16[256,128]{1,0:T(8,128)(2,1)} %param.8), channel_id=1, source_target_pairs={{0,8},{8,16},{16,24},{24,0},{1,9},{9,17},{17,25},{25,1},{2,10},{10... | collective-permute-start | bytes 196616 | tf_op jit(solution)/shard_map/ppermute | solution.py:14
  5.1 1.4 %collective-permute-start = (bf16[256,128]{1,0:T(8,128)(2,1)}, bf16[256,128]{1,0:T(8,128)(2,1)S(1)}, u32[]{:S(2)}, u32[]{:S(2)}) collective-permute-start(bf16[256,128]{1,0:T(8,128)(2,1)} %param.8), channel_id=1, source_target_pairs={{0,1},{1,2},{2,3},{3,4},{4,5},{5,6},{6,7},{7,0},{8,9},{9,10},{10,1... | collective-permute-start | bytes 196616 | tf_op jit(solution)/shard_map/ppermute | solution.py:14
  6.5 1.5 %copy.75 = bf16[32,8,16,128]{3,2,1,0:T(8,128)(2,1)S(1)} copy(bf16[32,8,16,128]{3,1,2,0:T(8,128)(2,1)} %bitcast.268) | data formatting | bytes 2097152
  8.0 1.5 %convert_bitcast_fusion = f32[32,8,16,128]{3,1,2,0:T(8,128)S(1)} fusion(bf16[256,2048]{1,0:T(8,128)(2,1)} %param.11), kind=kLoop, calls=%fused_computation.28 | loop fusion | flops 524288 | bytes 3145728
  9.5 0.4 copy.76
  9.9 0.6 %multiply_reduce_fusion = f32[256,16]{1,0:T(8,128)S(1)} fusion(f32[256,16,128]{2,1,0:T(8,128)S(1)} %bitcast.265, bf16[256,16,128]{2,1,0:T(8,128)(2,1)S(1)} %bitcast.267), kind=kLoop, calls=%fused_computation.30 | loop fusion | flops 1568768 | bytes 3162112 | tf_op jit(solution)/shard_map/reduce_sum | solution.py:52
  10.6 2.7 %fusion.70 = f32[256,256,16]{1,0,2:T(8,128)} fusion(bf16[256,128]{1,0:T(8,128)(2,1)S(1)} %copy-done.3, bf16[256,2048]{1,0:T(8,128)(2,1)S(1)} %copy-done), kind=kOutput, calls=%fused_computation.69 | convolution fusion | flops 268435456 | bytes 5308416 | tf_op jit(solution)/shard_map/qgd,kd->gqk/dot_general | solution.py:21
  13.3 0.2 multiply_reduce_fusion.1
  13.5 0.1 add_bitcast_fusion
  13.7 0.2 broadcast_compare_fusion
  13.9 3.7 %fusion.13 = bf16[16,256,256]{1,2,0:T(8,128)(2,1)S(1)} fusion(f32[256,256,16]{1,0,2:T(8,128)} %fusion.70, f32[16,256]{1,0:T(8,128)S(1)} %copy.37, f32[16,256]{1,0:T(8,128)S(1)} %copy-done.6, pred[256,256]{0,1:T(8,128)(4,1)S(1)} %get-tuple-element.15, bf16[256,128]{1,0:T(8,128)(2,1)S(1)} %copy-done.5, bf16[256,2048]{1,0:T(8,128)(2,1)S(1)} %copy-done.2), kind=kOutput, calls=%fused_computation.20 | convolution fusion | flops 274726912 | bytes 7503872 | tf_op jit(solution)/shard_map/qgd,kd->gqk/dot_general | solution.py:26
  17.7 0.7 %fusion.44 = bf16[256,128]{1,0:T(8,128)(2,1)S(1)} fusion(bf16[16,256,256]{1,2,0:T(8,128)(2,1)S(1)} %fusion.13, bf16[256,2048]{1,0:T(8,128)(2,1)S(1)} %copy-done), kind=kOutput, calls=%fused_computation.47 | convolution fusion | flops 268468224 | bytes 3211264 | tf_op jit(solution)/shard_map/gqk,qgd->kd/dot_general | solution.py:35
  18.4 0.3 collective-permute-start.6
  18.7 1.1 %fusion.49 = bf16[256,128]{1,0:T(8,128)(2,1)S(1)} fusion(f32[256,256,16]{1,0,2:T(8,128)S(1)} %copy-done.1, f32[16,256]{1,0:T(8,128)S(1)} %copy-done.6, pred[256,256]{0,1:T(8,128)(4,1)S(1)} %get-tuple-element.15, bf16[256,2048]{1,0:T(8,128)(2,1)S(1)} %copy-done.2), kind=kOutput, calls=%fused_computation.50 | convolution fusion | flops 272662528 | bytes 5390336 | tf_op jit(solution)/shard_map/gqk,qgd->kd/dot_general | solution.py:32
  19.8 0.5 fusion.100
  20.3 1.5 %collective-permute-start.11 = (bf16[256,128]{1,0:T(8,128)(2,1)S(1)}, bf16[256,128]{1,0:T(8,128)(2,1)S(1)}, u32[]{:S(2)}, u32[]{:S(2)}) collective-permute-start(bf16[256,128]{1,0:T(8,128)(2,1)S(1)} %fusion.49), channel_id=1, source_target_pairs={{0,1},{1,2},{2,3},{3,4},{4,5},{5,6},{6,7},{7,0},{8,9},{9,10},{10,1... | collective-permute-start | bytes 196616 | tf_op jit(solution)/shard_map/ppermute | solution.py:14
  21.8 0.7 %fusion.66 = f32[256,256,16]{1,0,2:T(8,128)S(1)} fusion(bf16[256,128]{1,0:T(8,128)(2,1)S(1)} %collective-permute-done.2, bf16[256,2048]{1,0:T(8,128)(2,1)S(1)} %copy-done), kind=kOutput, calls=%fused_computation.65 | convolution fusion | flops 268435456 | bytes 5308416 | tf_op jit(solution)/shard_map/qgd,kd->gqk/dot_general | solution.py:21
  22.5 1.1 %fusion.46 = bf16[256,128]{1,0:T(8,128)(2,1)S(1)} fusion(f32[256,256,16]{1,0,2:T(8,128)S(1)} %fusion.66, f32[16,256]{1,0:T(8,128)S(1)} %copy-done.6, pred[256,256]{0,1:T(8,128)(4,1)S(1)} %get-tuple-element.14, bf16[256,2048]{1,0:T(8,128)(2,1)S(1)} %copy-done.2), kind=kOutput, calls=%fused_computation.49 | convolution fusion | flops 272662528 | bytes 5390336 | tf_op jit(solution)/shard_map/gqk,qgd->kd/dot_general | solution.py:32
  23.6 1.5 %fusion.5 = bf16[16,256,256]{1,2,0:T(8,128)(2,1)S(1)} fusion(f32[256,256,16]{1,0,2:T(8,128)S(1)} %fusion.66, f32[16,256]{1,0:T(8,128)S(1)} %copy.37, f32[16,256]{1,0:T(8,128)S(1)} %copy-done.6, pred[256,256]{0,1:T(8,128)(4,1)S(1)} %get-tuple-element.14, bf16[256,128]{1,0:T(8,128)(2,1)S(1)} %collective-permute-done.3, bf16[256,2048]{1,0:T(8,128)(2,1)S(1)} %copy-done.2), kind=kOutput, calls=%fused_computation.8 | convolution fusion | flops 274726912 | bytes 7503872 | tf_op jit(solution)/shard_map/qgd,kd->gqk/dot_general | solution.py:26
  25.1 0.7 %fusion.45 = bf16[256,128]{1,0:T(8,128)(2,1)S(1)} fusion(bf16[16,256,256]{1,2,0:T(8,128)(2,1)S(1)} %fusion.5, bf16[256,2048]{1,0:T(8,128)(2,1)S(1)} %copy-done), kind=kOutput, calls=%fused_computation.48 | convolution fusion | flops 268468224 | bytes 3211264 | tf_op jit(solution)/shard_map/gqk,qgd->kd/dot_general | solution.py:35
  25.8 0.3 collective-permute-start.8
  26.1 1.4 %collective-permute-start.13 = (bf16[256,128]{1,0:T(8,128)(2,1)S(1)}, bf16[256,128]{1,0:T(8,128)(2,1)S(1)}, u32[]{:S(2)}, u32[]{:S(2)}) collective-permute-start(bf16[256,128]{1,0:T(8,128)(2,1)S(1)} %fusion.46), channel_id=1, source_target_pairs={{0,1},{1,2},{2,3},{3,4},{4,5},{5,6},{6,7},{7,0},{8,9},{9,10},{10,1... | collective-permute-start | bytes 196616 | tf_op jit(solution)/shard_map/ppermute | solution.py:14
  27.5 0.7 %fusion.68 = f32[256,256,16]{1,0,2:T(8,128)S(1)} fusion(bf16[256,128]{1,0:T(8,128)(2,1)S(1)} %collective-permute-done, bf16[256,2048]{1,0:T(8,128)(2,1)S(1)} %copy-done), kind=kOutput, calls=%fused_computation.67 | convolution fusion | flops 268435456 | bytes 5308416 | tf_op jit(solution)/shard_map/qgd,kd->gqk/dot_general | solution.py:21
  28.2 1.1 %convert_add_fusion.1 = f32[256,128]{1,0:T(8,128)S(1)} fusion(bf16[256,128]{1,0:T(8,128)(2,1)S(1)} %collective-permute-done.11, f32[256,256,16]{1,0,2:T(8,128)S(1)} %fusion.68, f32[16,256]{1,0:T(8,128)S(1)} %copy-done.6, pred[256,256]{0,1:T(8,128)(4,1)S(1)} %get-tuple-element.16, bf16[256,2048]{1,0:T(8,128)(2,1)S(1)} %copy-done.2), kind=kOutput, calls=%fused_computation.88 | convolution fusion | flops 272695296 | bytes 5521408 | tf_op jit(solution)/shard_map/gqk,qgd->kd/dot_general | solution.py:32
  29.3 2.4 %collective-permute-start.12 = (f32[256,128]{1,0:T(8,128)S(1)}, f32[256,128]{1,0:T(8,128)S(1)}, u32[]{:S(2)}, u32[]{:S(2)}) collective-permute-start(f32[256,128]{1,0:T(8,128)S(1)} %convert_add_fusion.1), channel_id=1, source_target_pairs={{0,7},{1,0},{2,1},{3,2},{4,3},{5,4},{6,5},{7,6},{8,15},{9,8},{10,9... | collective-permute-start | bytes 393224 | tf_op jit(solution)/shard_map/ppermute | solution.py:14
  31.7 1.5 %fusion.9 = bf16[16,256,256]{1,2,0:T(8,128)(2,1)S(1)} fusion(f32[256,256,16]{1,0,2:T(8,128)S(1)} %fusion.68, f32[16,256]{1,0:T(8,128)S(1)} %copy.37, f32[16,256]{1,0:T(8,128)S(1)} %copy-done.6, pred[256,256]{0,1:T(8,128)(4,1)S(1)} %get-tuple-element.16, bf16[256,128]{1,0:T(8,128)(2,1)S(1)} %collective-permute-done.1, bf16[256,2048]{1,0:T(8,128)(2,1)S(1)} %copy-done.2), kind=kOutput, calls=%fused_computation.14 | convolution fusion | flops 274726912 | bytes 7503872 | tf_op jit(solution)/shard_map/qgd,kd->gqk/dot_general | solution.py:26
  33.2 0.7 %convert_add_fusion.3 = f32[256,128]{1,0:T(8,128)S(1)} fusion(bf16[256,128]{1,0:T(8,128)(2,1)S(1)} %collective-permute-done.6, bf16[16,256,256]{1,2,0:T(8,128)(2,1)S(1)} %fusion.9, bf16[256,2048]{1,0:T(8,128)(2,1)S(1)} %copy-done), kind=kOutput, calls=%fused_computation.91 | convolution fusion | flops 268500992 | bytes 3342336 | tf_op jit(solution)/shard_map/gqk,qgd->kd/dot_general | solution.py:35
  33.9 0.3 collective-permute-start.7
  34.2 0.3 collective-permute-start.4
  34.5 0.5 fusion.96
  34.9 4.7 %collective-permute-done.4 = bf16[256,128]{1,0:T(8,128)(2,1)S(1)} collective-permute-done((bf16[256,128]{1,0:T(8,128)(2,1)S(1)}, bf16[256,128]{1,0:T(8,128)(2,1)S(1)}, u32[]{:S(2)}, u32[]{:S(2)}) %collective-permute-start.4) | collective-permute-done | bytes 65568 | tf_op jit(solution)/shard_map/ppermute | solution.py:14
  39.7 0.7 %fusion.64 = f32[256,256,16]{1,0,2:T(8,128)S(1)} fusion(bf16[256,128]{1,0:T(8,128)(2,1)S(1)} %collective-permute-done.4, bf16[256,2048]{1,0:T(8,128)(2,1)S(1)} %copy-done), kind=kOutput, calls=%fused_computation.63 | convolution fusion | flops 268435456 | bytes 5308416 | tf_op jit(solution)/shard_map/qgd,kd->gqk/dot_general | solution.py:21
  40.4 1.1 %convert_add_fusion = f32[256,128]{1,0:T(8,128)S(1)} fusion(bf16[256,128]{1,0:T(8,128)(2,1)S(1)} %collective-permute-done.13, f32[256,256,16]{1,0,2:T(8,128)S(1)} %fusion.64, f32[16,256]{1,0:T(8,128)S(1)} %copy-done.6, pred[256,256]{0,1:T(8,128)(4,1)S(1)} %get-tuple-element.13, bf16[256,2048]{1,0:T(8,128)(2,1)S(1)} %copy-done.2), kind=kOutput, calls=%fused_computation.87 | convolution fusion | flops 272695296 | bytes 5521408 | tf_op jit(solution)/shard_map/gqk,qgd->kd/dot_general | solution.py:32
  41.5 3.6 %collective-permute-start.14 = (f32[256,128]{1,0:T(8,128)S(1)}, f32[256,128]{1,0:T(8,128)S(1)}, u32[]{:S(2)}, u32[]{:S(2)}) collective-permute-start(f32[256,128]{1,0:T(8,128)S(1)} %convert_add_fusion), channel_id=1, source_target_pairs={{0,7},{1,0},{2,1},{3,2},{4,3},{5,4},{6,5},{7,6},{8,15},{9,8},{10,9... | collective-permute-start | bytes 393224 | tf_op jit(solution)/shard_map/ppermute | solution.py:14
  45.1 0.8 %collective-permute-done.5 = bf16[256,128]{1,0:T(8,128)(2,1)S(1)} collective-permute-done((bf16[256,128]{1,0:T(8,128)(2,1)S(1)}, bf16[256,128]{1,0:T(8,128)(2,1)S(1)}, u32[]{:S(2)}, u32[]{:S(2)}) %collective-permute-start.5) | collective-permute-done | bytes 65568 | tf_op jit(solution)/shard_map/ppermute | solution.py:14
  45.9 1.5 %fusion.1 = bf16[16,256,256]{1,2,0:T(8,128)(2,1)S(1)} fusion(f32[256,256,16]{1,0,2:T(8,128)S(1)} %fusion.64, f32[16,256]{1,0:T(8,128)S(1)} %copy.37, f32[16,256]{1,0:T(8,128)S(1)} %copy-done.6, pred[256,256]{0,1:T(8,128)(4,1)S(1)} %get-tuple-element.13, bf16[256,128]{1,0:T(8,128)(2,1)S(1)} %collective-permute-done.5, bf16[256,2048]{1,0:T(8,128)(2,1)S(1)} %copy-done.2), kind=kOutput, calls=%fused_computation.2 | convolution fusion | flops 274726912 | bytes 7503872 | tf_op jit(solution)/shard_map/qgd,kd->gqk/dot_general | solution.py:26
  47.3 0.7 %convert_add_fusion.2 = f32[256,128]{1,0:T(8,128)S(1)} fusion(bf16[256,128]{1,0:T(8,128)(2,1)S(1)} %collective-permute-done.8, bf16[16,256,256]{1,2,0:T(8,128)(2,1)S(1)} %fusion.1, bf16[256,2048]{1,0:T(8,128)(2,1)S(1)} %copy-done), kind=kOutput, calls=%fused_computation.90 | convolution fusion | flops 268500992 | bytes 3342336 | tf_op jit(solution)/shard_map/gqk,qgd->kd/dot_general | solution.py:35
  48.1 0.5 fusion.92
  48.7 1.5 %collective-permute-start.15 = (f32[256,128]{1,0:T(8,128)S(1)}, f32[256,128]{1,0:T(8,128)S(1)}, u32[]{:S(2)}, u32[]{:S(2)}) collective-permute-start(f32[256,128]{1,0:T(8,128)S(1)} %collective-permute-done.14), channel_id=1, source_target_pairs={{0,24},{8,0},{16,8},{24,16},{1,25},{9,1},{17,9},{25,17},{2,26},{10... | collective-permute-start | bytes 393224 | tf_op jit(solution)/shard_map/ppermute | solution.py:14
  50.1 0.5 collective-permute-done.9
  50.7 1.4 %collective-permute-start.10 = (f32[256,128]{1,0:T(8,128)S(1)}, f32[256,128]{1,0:T(8,128)S(1)}, u32[]{:S(2)}, u32[]{:S(2)}) collective-permute-start(f32[256,128]{1,0:T(8,128)S(1)} %collective-permute-done.9), channel_id=1, source_target_pairs={{0,24},{8,0},{16,8},{24,16},{1,25},{9,1},{17,9},{25,17},{2,26},{10... | collective-permute-start | bytes 393224 | tf_op jit(solution)/shard_map/ppermute | solution.py:14
  52.1 1.0 %multiply_convert_fusion = bf16[16,256,128]{1,2,0:T(8,128)(2,1)S(1)} fusion(f32[16,256,128]{1,2,0:T(8,128)S(1)} %fusion.92, f32[16,256,128]{1,2,0:T(8,128)S(1)} %fusion.100, f32[16,256,128]{1,2,0:T(8,128)S(1)} %fusion.96, bf16[16,256,256]{1,2,0:T(8,128)(2,1)S(1)} %fusion.1, bf16[256,128]{1,0:T(8,128)(2,1)S(1)} %collective-permute-done.4), kind=kOutput, calls=%fused_computation.29 | convolution fusion | flops 271056896 | bytes 9502720 | tf_op jit(solution)/shard_map/gqk,kd->qgd/dot_general | solution.py:38
  53.1 1.4 %copy.60 = bf16[256,2048]{1,0:T(8,128)(2,1)} copy(bf16[256,2048]{0,1:T(8,128)(2,1)S(1)} %bitcast.266) | data formatting | bytes 2097152
  54.5 0.5 collective-permute-done.15
  55.0 0.7 %add.204 = f32[256,128]{1,0:T(8,128)} add(f32[256,128]{1,0:T(8,128)S(1)} %collective-permute-done.12, f32[256,128]{1,0:T(8,128)S(1)} %collective-permute-done.15) | non-fusion elementwise | flops 32768 | bytes 393216 | tf_op jit(solution)/shard_map/add | solution.py:107
  55.7 1.7 %collective-permute-done.10 = f32[256,128]{1,0:T(8,128)S(1)} collective-permute-done((f32[256,128]{1,0:T(8,128)S(1)}, f32[256,128]{1,0:T(8,128)S(1)}, u32[]{:S(2)}, u32[]{:S(2)}) %collective-permute-start.10) | collective-permute-done | bytes 131104 | tf_op jit(solution)/shard_map/ppermute | solution.py:14
  57.4 0.7 %add_multiply_fusion = f32[256,128]{1,0:T(8,128)} fusion(f32[256,128]{1,0:T(8,128)S(1)} %collective-permute-done.7, f32[256,128]{1,0:T(8,128)S(1)} %collective-permute-done.10), kind=kLoop, calls=%fused_computation.89 | loop fusion | flops 65536 | bytes 393216 | tf_op jit(solution)/shard_map/mul | solution.py:111
  (30 shorter events, 0.3 us)
Async XLA Ops:
  0.6 10.0 %copy-start = (bf16[256,2048]{1,0:T(8,128)(2,1)S(1)}, bf16[256,2048]{1,0:T(8,128)(2,1)}, u32[]{:S(2)}) copy-start(bf16[256,2048]{1,0:T(8,128)(2,1)} %param.7) | copy-start | bytes 3145732
  0.6 22.9 %collective-permute-start.3 = (bf16[256,128]{1,0:T(8,128)(2,1)}, bf16[256,128]{1,0:T(8,128)(2,1)S(1)}, u32[]{:S(2)}, u32[]{:S(2)}) collective-permute-start(bf16[256,128]{1,0:T(8,128)(2,1)} %param.9), channel_id=1, source_target_pairs={{0,8},{8,16},{16,24},{24,0},{1,9},{9,17},{17,25},{25,1},{2,10},{10... | collective-permute-start | bytes 196616 | tf_op jit(solution)/shard_map/ppermute | solution.py:14
  3.6 28.0 %collective-permute-start.1 = (bf16[256,128]{1,0:T(8,128)(2,1)}, bf16[256,128]{1,0:T(8,128)(2,1)S(1)}, u32[]{:S(2)}, u32[]{:S(2)}) collective-permute-start(bf16[256,128]{1,0:T(8,128)(2,1)} %param.9), channel_id=1, source_target_pairs={{0,1},{1,2},{2,3},{3,4},{4,5},{5,6},{6,7},{7,0},{8,9},{9,10},{10,1... | collective-permute-start | bytes 196616 | tf_op jit(solution)/shard_map/ppermute | solution.py:14
  3.6 16.7 %collective-permute-start.2 = (bf16[256,128]{1,0:T(8,128)(2,1)}, bf16[256,128]{1,0:T(8,128)(2,1)S(1)}, u32[]{:S(2)}, u32[]{:S(2)}) collective-permute-start(bf16[256,128]{1,0:T(8,128)(2,1)} %param.8), channel_id=1, source_target_pairs={{0,8},{8,16},{16,24},{24,0},{1,9},{9,17},{17,25},{25,1},{2,10},{10... | collective-permute-start | bytes 196616 | tf_op jit(solution)/shard_map/ppermute | solution.py:14
  5.1 21.0 %collective-permute-start = (bf16[256,128]{1,0:T(8,128)(2,1)}, bf16[256,128]{1,0:T(8,128)(2,1)S(1)}, u32[]{:S(2)}, u32[]{:S(2)}) collective-permute-start(bf16[256,128]{1,0:T(8,128)(2,1)} %param.8), channel_id=1, source_target_pairs={{0,1},{1,2},{2,3},{3,4},{4,5},{5,6},{6,7},{7,0},{8,9},{9,10},{10,1... | collective-permute-start | bytes 196616 | tf_op jit(solution)/shard_map/ppermute | solution.py:14
  9.5 1.1 %copy-start.3 = (bf16[256,128]{1,0:T(8,128)(2,1)S(1)}, bf16[256,128]{1,0:T(8,128)(2,1)}, u32[]{:S(2)}) copy-start(bf16[256,128]{1,0:T(8,128)(2,1)} %param.8) | copy-start | bytes 196612
  9.9 3.4 %copy-start.4 = (s32[32,2]{0,1:T(2,128)S(1)}, s32[32,2]{0,1:T(2,128)}, u32[]{:S(2)}) copy-start(s32[32,2]{0,1:T(2,128)} %param.13) | copy-start | bytes 772
  9.9 4.0 %copy-start.2 = (bf16[256,2048]{1,0:T(8,128)(2,1)S(1)}, bf16[256,2048]{1,0:T(8,128)(2,1)}, u32[]{:S(2)}) copy-start(bf16[256,2048]{1,0:T(8,128)(2,1)} %param.10) | copy-start | bytes 3145732
  9.9 4.0 %copy-start.5 = (bf16[256,128]{1,0:T(8,128)(2,1)S(1)}, bf16[256,128]{1,0:T(8,128)(2,1)}, u32[]{:S(2)}) copy-start(bf16[256,128]{1,0:T(8,128)(2,1)} %param.9) | copy-start | bytes 196612
  9.9 4.0 %copy-start.6 = (f32[16,256]{1,0:T(8,128)S(1)}, f32[16,256]{1,0:T(8,128)}, u32[]{:S(2)}) copy-start(f32[16,256]{1,0:T(8,128)} %param.12) | copy-start | bytes 49156
  13.9 4.8 %copy-start.1 = (f32[256,256,16]{1,0,2:T(8,128)S(1)}, f32[256,256,16]{1,0,2:T(8,128)}, u32[]{:S(2)}) copy-start(f32[256,256,16]{1,0,2:T(8,128)} %fusion.70) | copy-start | bytes 12582916
  18.4 14.8 %collective-permute-start.6 = (bf16[256,128]{1,0:T(8,128)(2,1)S(1)}, bf16[256,128]{1,0:T(8,128)(2,1)S(1)}, u32[]{:S(2)}, u32[]{:S(2)}) collective-permute-start(bf16[256,128]{1,0:T(8,128)(2,1)S(1)} %fusion.44), channel_id=1, source_target_pairs={{0,1},{1,2},{2,3},{3,4},{4,5},{5,6},{6,7},{7,0},{8,9},{9,10},{10,1... | collective-permute-start | bytes 196616 | tf_op jit(solution)/shard_map/ppermute | solution.py:14
  20.3 7.9 %collective-permute-start.11 = (bf16[256,128]{1,0:T(8,128)(2,1)S(1)}, bf16[256,128]{1,0:T(8,128)(2,1)S(1)}, u32[]{:S(2)}, u32[]{:S(2)}) collective-permute-start(bf16[256,128]{1,0:T(8,128)(2,1)S(1)} %fusion.49), channel_id=1, source_target_pairs={{0,1},{1,2},{2,3},{3,4},{4,5},{5,6},{6,7},{7,0},{8,9},{9,10},{10,1... | collective-permute-start | bytes 196616 | tf_op jit(solution)/shard_map/ppermute | solution.py:14
  25.8 21.6 %collective-permute-start.8 = (bf16[256,128]{1,0:T(8,128)(2,1)S(1)}, bf16[256,128]{1,0:T(8,128)(2,1)S(1)}, u32[]{:S(2)}, u32[]{:S(2)}) collective-permute-start(bf16[256,128]{1,0:T(8,128)(2,1)S(1)} %fusion.45), channel_id=1, source_target_pairs={{0,1},{1,2},{2,3},{3,4},{4,5},{5,6},{6,7},{7,0},{8,9},{9,10},{10,1... | collective-permute-start | bytes 196616 | tf_op jit(solution)/shard_map/ppermute | solution.py:14
  26.1 14.3 %collective-permute-start.13 = (bf16[256,128]{1,0:T(8,128)(2,1)S(1)}, bf16[256,128]{1,0:T(8,128)(2,1)S(1)}, u32[]{:S(2)}, u32[]{:S(2)}) collective-permute-start(bf16[256,128]{1,0:T(8,128)(2,1)S(1)} %fusion.46), channel_id=1, source_target_pairs={{0,1},{1,2},{2,3},{3,4},{4,5},{5,6},{6,7},{7,0},{8,9},{9,10},{10,1... | collective-permute-start | bytes 196616 | tf_op jit(solution)/shard_map/ppermute | solution.py:14
  29.3 25.2 %collective-permute-start.12 = (f32[256,128]{1,0:T(8,128)S(1)}, f32[256,128]{1,0:T(8,128)S(1)}, u32[]{:S(2)}, u32[]{:S(2)}) collective-permute-start(f32[256,128]{1,0:T(8,128)S(1)} %convert_add_fusion.1), channel_id=1, source_target_pairs={{0,7},{1,0},{2,1},{3,2},{4,3},{5,4},{6,5},{7,6},{8,15},{9,8},{10,9... | collective-permute-start | bytes 393224 | tf_op jit(solution)/shard_map/ppermute | solution.py:14
  33.9 21.8 %collective-permute-start.7 = (f32[256,128]{1,0:T(8,128)S(1)}, f32[256,128]{1,0:T(8,128)S(1)}, u32[]{:S(2)}, u32[]{:S(2)}) collective-permute-start(f32[256,128]{1,0:T(8,128)S(1)} %convert_add_fusion.3), channel_id=1, source_target_pairs={{0,7},{1,0},{2,1},{3,2},{4,3},{5,4},{6,5},{7,6},{8,15},{9,8},{10,9... | collective-permute-start | bytes 393224 | tf_op jit(solution)/shard_map/ppermute | solution.py:14
  34.2 5.5 %collective-permute-start.4 = (bf16[256,128]{1,0:T(8,128)(2,1)S(1)}, bf16[256,128]{1,0:T(8,128)(2,1)S(1)}, u32[]{:S(2)}, u32[]{:S(2)}) collective-permute-start(bf16[256,128]{1,0:T(8,128)(2,1)S(1)} %collective-permute-done.2), channel_id=1, source_target_pairs={{0,1},{1,2},{2,3},{3,4},{4,5},{5,6},{6,7},{7,0},{8,9},{9,10},{10,1... | collective-permute-start | bytes 196616 | tf_op jit(solution)/shard_map/ppermute | solution.py:14
  39.7 6.2 %collective-permute-start.5 = (bf16[256,128]{1,0:T(8,128)(2,1)S(1)}, bf16[256,128]{1,0:T(8,128)(2,1)S(1)}, u32[]{:S(2)}, u32[]{:S(2)}) collective-permute-start(bf16[256,128]{1,0:T(8,128)(2,1)S(1)} %collective-permute-done.3), channel_id=1, source_target_pairs={{0,1},{1,2},{2,3},{3,4},{4,5},{5,6},{6,7},{7,0},{8,9},{9,10},{10,1... | collective-permute-start | bytes 196616 | tf_op jit(solution)/shard_map/ppermute | solution.py:14
  41.5 7.2 %collective-permute-start.14 = (f32[256,128]{1,0:T(8,128)S(1)}, f32[256,128]{1,0:T(8,128)S(1)}, u32[]{:S(2)}, u32[]{:S(2)}) collective-permute-start(f32[256,128]{1,0:T(8,128)S(1)} %convert_add_fusion), channel_id=1, source_target_pairs={{0,7},{1,0},{2,1},{3,2},{4,3},{5,4},{6,5},{7,6},{8,15},{9,8},{10,9... | collective-permute-start | bytes 393224 | tf_op jit(solution)/shard_map/ppermute | solution.py:14
  48.1 2.6 %collective-permute-start.9 = (f32[256,128]{1,0:T(8,128)S(1)}, f32[256,128]{1,0:T(8,128)S(1)}, u32[]{:S(2)}, u32[]{:S(2)}) collective-permute-start(f32[256,128]{1,0:T(8,128)S(1)} %convert_add_fusion.2), channel_id=1, source_target_pairs={{0,7},{1,0},{2,1},{3,2},{4,3},{5,4},{6,5},{7,6},{8,15},{9,8},{10,9... | collective-permute-start | bytes 393224 | tf_op jit(solution)/shard_map/ppermute | solution.py:14
  48.7 6.3 %collective-permute-start.15 = (f32[256,128]{1,0:T(8,128)S(1)}, f32[256,128]{1,0:T(8,128)S(1)}, u32[]{:S(2)}, u32[]{:S(2)}) collective-permute-start(f32[256,128]{1,0:T(8,128)S(1)} %collective-permute-done.14), channel_id=1, source_target_pairs={{0,24},{8,0},{16,8},{24,16},{1,25},{9,1},{17,9},{25,17},{2,26},{10... | collective-permute-start | bytes 393224 | tf_op jit(solution)/shard_map/ppermute | solution.py:14
  50.7 6.7 %collective-permute-start.10 = (f32[256,128]{1,0:T(8,128)S(1)}, f32[256,128]{1,0:T(8,128)S(1)}, u32[]{:S(2)}, u32[]{:S(2)}) collective-permute-start(f32[256,128]{1,0:T(8,128)S(1)} %collective-permute-done.9), channel_id=1, source_target_pairs={{0,24},{8,0},{16,8},{24,16},{1,25},{9,1},{17,9},{25,17},{2,26},{10... | collective-permute-start | bytes 393224 | tf_op jit(solution)/shard_map/ppermute | solution.py:14
where the time goes:
time: 58.3 us; the launch traced here: 58.1 us
  matrix products  22.5 us (39%)
  starting transfers between devices  18.9 us (32%)
  waiting for transfers between devices  8.3 us (14%)
  other arithmetic  4 us (7%)
  local copies, waits for them, and re-layouts  3.36 us (6%)
  between operations  0.93 us (2%)
    ppermute x16, starting transfers between devices, shifted(): lax.ppermute(shard, axis, [(i, (i + by) % devices) for i in range(devices)])  18.9 us
    ppermute x16, waiting for transfers between devices, shifted(): lax.ppermute(shard, axis, [(i, (i + by) % devices) for i in range(devices)])  8.3 us
    dot_general x4, matrix products, block_grads(): jnp.einsum('qgd,kd->gqk', grad_block, value_block, preferred_element_type...  8.14 us
    dot_general x4, matrix products, block_grads(): jnp.einsum('qgd,kd->gqk', query_block, key_block, preferred_element_type=...  4.81 us
    dot_general x4, matrix products, block_grads(): jnp.einsum('gqk,qgd->kd', weights_low, grad_block, preferred_element_type...  4.27 us
    unnamed x17, local copies, waits for them, and re-layouts  3.3 us
    dot_general x4, matrix products, block_grads(): jnp.einsum('gqk,qgd->kd', dscores_low, query_block, preferred_element_typ...  2.89 us
    dot_general x4, matrix products, block_grads(): jnp.einsum('gqk,kd->qgd', dscores_low, key_block, preferred_element_type=...  2.43 us
  transfers between devices with their start and end apart: 16, of which 5 were waited for; matrix products, arithmetic and copies ran while one was open for 50% of the time, Pallas kernels for 0%

commit v1 on v0

v1 whole, which is shorter than its diff:
```python
import functools
import math

import jax
import jax.numpy as jnp
from jax import lax
from jax.experimental import pallas as pl
from jax.experimental.pallas import tpu as pltpu
from jax.sharding import PartitionSpec as P

MESH = pl.DeviceIdType.MESH
HD = 128
LOG2E = 1.4426950408889634
F32 = jnp.float32
BF16 = jnp.bfloat16

STEPS = ((0, 1), (1, 0), (1, 1))
SEND_ORDER = (1, 2, 0)


def dot_nt(a, b):
    return lax.dot_general(a, b, (((1,), (1,)), ((), ())), preferred_element_type=F32)


def dot(a, b):
    return jnp.dot(a, b, preferred_element_type=F32)


def kernel(
    outer_count, inner_count, heads,
    span_ref, q_hbm, k_hbm, v_hbm, do_hbm, o_hbm, lse_hbm,
    dq_hbm, dk_ref, dv_ref,
    q, do, o, own_k, own_v, lse, lse2, rdot,
    kin_a, kin_b, kin_c, vin_a, vin_b, vin_c, pin, pout, p_t, ds_t, dq_l, dq_stage,
    in_sem, ks_send, ks_recv, vs_send, vs_recv, ps_send, ps_recv, out_sem,
):
    me_o = lax.axis_index("outer")
    me_i = lax.axis_index("inner")
    pairs = heads // 2
    factor = 1.0 / math.sqrt(HD)
    kin, vin = (kin_a, kin_b, kin_c), (vin_a, vin_b, vin_c)

    loads = [
        pltpu.make_async_copy(src, dst, in_sem.at[n])
        for n, (src, dst) in enumerate(
            ((lse_hbm, lse), (k_hbm, own_k), (v_hbm, own_v), (do_hbm, do), (o_hbm, o), (q_hbm, q))
        )
    ]
    for load in loads:
        load.start()

    def ahead(step):
        return (lax.rem(me_o + step[0], outer_count), lax.rem(me_i + step[1], inner_count))

    def behind(step):
        return (
            lax.rem(me_o + outer_count - step[0], outer_count),
            lax.rem(me_i + inner_count - step[1], inner_count),
        )

    barrier = pltpu.get_barrier_semaphore()
    for step in STEPS:
        pl.semaphore_signal(barrier, inc=1, device_id=ahead(step), device_id_type=MESH)
        pl.semaphore_signal(barrier, inc=1, device_id=behind(step), device_id_type=MESH)
    pl.semaphore_wait(barrier, 2 * len(STEPS))

    k_copies, v_copies = {}, {}
    for j in SEND_ORDER:
        for table, src, dst, ssem, rsem in (
            (k_copies, k_hbm, kin, ks_send, ks_recv),
            (v_copies, v_hbm, vin, vs_send, vs_recv),
        ):
            table[j] = pltpu.make_async_remote_copy(
                src_ref=src, dst_ref=dst[j], send_sem=ssem.at[j], recv_sem=rsem.at[j],
                device_id=ahead(STEPS[j]), device_id_type=MESH,
            )
            table[j].start()

    def cols(h):
        return slice(h * HD, (h + 1) * HD)

    def pair_rows(ref, half, p):
        return jnp.concatenate([ref[half, :, cols(2 * p)], ref[half, :, cols(2 * p + 1)]], axis=0)

    def all_rows(ref, half):
        return jnp.concatenate([ref[half, :, cols(h)] for h in range(heads)], axis=0)

    def pair_lanes(ref, half, p):
        return jnp.concatenate(
            [ref[half, 2 * p : 2 * p + 1, :], ref[half, 2 * p + 1 : 2 * p + 2, :]], axis=1
        )

    for load in loads[:5]:
        load.wait()
    for s in range(2):
        lse2[s] = lse[:, s * HD : (s + 1) * HD] * LOG2E
    ones = jnp.ones((16, 2 * HD), BF16)
    for s in range(2):
        for p in range(pairs):
            terms = []
            for h in (2 * p, 2 * p + 1):
                prod = do[s, :, cols(h)].astype(F32) * o[s, :, cols(h)].astype(F32)
                high = prod.astype(BF16)
                low = (prod - high.astype(F32)).astype(BF16)
                terms.append(jnp.concatenate([high, low], axis=1))
            sums = dot_nt(ones, jnp.concatenate(terms, axis=0))
            rdot[s, 2 * p : 2 * p + 1, :] = sums[0:1, :HD]
            rdot[s, 2 * p + 1 : 2 * p + 2, :] = sums[0:1, HD:]
    loads[5].wait()

    scale2 = factor * LOG2E

    def weights(keys, values, half, p, mask):
        scores = dot_nt(keys, pair_rows(q, half, p))
        dprobs = dot_nt(values, pair_rows(do, half, p))
        probs = jnp.exp2(scores * scale2 - pair_lanes(lse2, half, p))
        if mask is not None:
            probs = jnp.where(mask, probs, 0.0)
        dscores = probs * (dprobs - pair_lanes(rdot, half, p))
        return probs.astype(BF16), dscores.astype(BF16)

    k_rows = lax.broadcasted_iota(jnp.int32, (HD, 2 * HD), 0)
    q_lanes = lax.broadcasted_iota(jnp.int32, (HD, 2 * HD), 1) % HD
    triangle = k_rows <= q_lanes
    lo_k, hi_k = own_k[0], own_k[1]
    lo_v, hi_v = own_v[0], own_v[1]
    for p in range(pairs):
        lanes = slice(2 * p * HD, (2 * p + 2) * HD)
        for row, keys, values, half, mask in (
            (0, lo_k, lo_v, 0, triangle), (1, lo_k, lo_v, 1, None), (2, hi_k, hi_v, 1, triangle)
        ):
            probs, dscores = weights(keys, values, half, p, mask)
            p_t[row * HD : (row + 1) * HD, lanes] = probs
            ds_t[row * HD : (row + 1) * HD, lanes] = dscores
    for out, lhs, rhs in ((dv_ref, p_t, do), (dk_ref, ds_t, q)):
        late = dot(lhs[HD : 3 * HD, :], all_rows(rhs, 1))
        out[0] = late[:HD] + dot(lhs[:HD, :], all_rows(rhs, 0))
        out[1] = late[HD:]

    zero = jnp.zeros((HD, HD), BF16)
    dq_l[0:HD, 0:HD] = zero
    dq_l[HD:, 0:HD] = lo_k.T
    dq_l[0:HD, HD : 2 * HD] = lo_k.T
    dq_l[0:HD, 2 * HD : 3 * HD] = hi_k.T
    dq_l[HD:, HD : 2 * HD] = zero
    dq_l[HD:, 2 * HD : 3 * HD] = zero

    me_span = span_ref[0, me_o * inner_count + me_i]
    p_copies = []
    for j, step in enumerate(STEPS):
        src_o, src_i = behind(step)
        src_span = span_ref[0, src_o * inner_count + src_i]
        early = src_span < me_span
        half = jnp.where(early, 0, 1)
        k_copies[j].wait_recv()
        v_copies[j].wait_recv()
        lo_k, sel_k = kin[j][0], kin[j][half]
        lo_v, sel_v = vin[j][0], vin[j][half]
        base = (3 + 2 * j) * HD
        for p in range(pairs):
            lanes = slice(2 * p * HD, (2 * p + 2) * HD)
            for row, keys, values, side in ((0, lo_k, lo_v, 1), (1, sel_k, sel_v, half)):
                probs, dscores = weights(keys, values, side, p, None)
                p_t[row * HD : (row + 1) * HD, lanes] = probs
                ds_t[base + row * HD : base + (row + 1) * HD, lanes] = dscores
        is_early = jnp.full((HD, HD), src_span, jnp.int32) < me_span
        for n, (lhs, at, rhs) in enumerate(((ds_t, base, q), (p_t, 0, do))):
            on_lo = dot(lhs[at : at + HD, :], all_rows(rhs, 1))
            on_sel = dot(lhs[at + HD : at + 2 * HD, :], all_rows(rhs, half))
            pout[j, 2 * n] = (on_lo + jnp.where(is_early, on_sel, 0.0)).astype(BF16)
            pout[j, 2 * n + 1] = jnp.where(is_early, 0.0, on_sel).astype(BF16)
        copy = pltpu.make_async_remote_copy(
            src_ref=pout.at[j], dst_ref=pin.at[j], send_sem=ps_send.at[j], recv_sem=ps_recv.at[j],
            device_id=behind(step), device_id_type=MESH,
        )
        copy.start()
        p_copies.append(copy)
        sel_t = sel_k.astype(F32).T
        dq_l[0:HD, base : base + HD] = lo_k.T
        dq_l[0:HD, base + HD : base + 2 * HD] = jnp.where(is_early, 0.0, sel_t).astype(BF16)
        dq_l[HD:, base : base + HD] = zero
        dq_l[HD:, base + HD : base + 2 * HD] = jnp.where(is_early, sel_t, 0.0).astype(BF16)

    stores = []
    for p in range(pairs):
        lanes = slice(2 * p * HD, (2 * p + 2) * HD)
        grads = dot(dq_l[...], ds_t[:, lanes]) * factor
        for s in range(2):
            for n in range(2):
                tile = grads[(1 - s) * HD : (2 - s) * HD, n * HD : (n + 1) * HD]
                dq_stage[s, :, cols(2 * p + n)] = tile.T.astype(BF16)
        store = pltpu.make_async_copy(
            dq_stage.at[:, :, lanes], dq_hbm.at[:, :, lanes], out_sem.at[p]
        )
        store.start()
        stores.append(store)

    for j in range(len(STEPS)):
        p_copies[j].wait_recv()
    for s in range(2):
        dk_ref[s] = (dk_ref[s] + sum(pin[j, s].astype(F32) for j in range(len(STEPS)))) * factor
        dv_ref[s] = dv_ref[s] + sum(pin[j, 2 + s].astype(F32) for j in range(len(STEPS)))
    for store in stores:
        store.wait()
    for j in range(len(STEPS)):
        k_copies[j].wait_send()
        v_copies[j].wait_send()
        p_copies[j].wait_send()


def per_device(outer_count, inner_count, queries, key_rows, value_rows, out_grad, outputs, log_sum, span_table):
    heads = log_sum.shape[0]
    rows, width = queries.shape
    half = rows // 2
    steps = len(STEPS)
    any_spec = pl.BlockSpec(memory_space=pl.ANY)
    vmem = pl.BlockSpec(memory_space=pltpu.VMEM)
    smem = pl.BlockSpec(memory_space=pltpu.SMEM)
    wide = (2, half, width)
    narrow = (2, half, HD)
    dma = pltpu.SemaphoreType.DMA
    dq, dk, dv = pl.pallas_call(
        functools.partial(kernel, outer_count, inner_count, heads),
        out_shape=(
            jax.ShapeDtypeStruct(wide, BF16),
            jax.ShapeDtypeStruct(narrow, F32),
            jax.ShapeDtypeStruct(narrow, F32),
        ),
        in_specs=[smem] + [any_spec] * 6,
        out_specs=(any_spec, vmem, vmem),
        scratch_shapes=[
            pltpu.VMEM(wide, BF16), pltpu.VMEM(wide, BF16), pltpu.VMEM(wide, BF16),
            pltpu.VMEM(narrow, BF16), pltpu.VMEM(narrow, BF16),
            pltpu.VMEM((heads, rows), F32), pltpu.VMEM((2, heads, half), F32), pltpu.VMEM((2, heads, half), F32),
            *[pltpu.VMEM(narrow, BF16) for _ in range(2 * steps)],
            pltpu.VMEM((steps, 4, half, HD), BF16), pltpu.VMEM((steps, 4, half, HD), BF16),
            pltpu.VMEM((3 * half, width), BF16),
            pltpu.VMEM(((3 + 2 * steps) * half, width), BF16),
            pltpu.VMEM((2 * HD, (3 + 2 * steps) * half), BF16),
            pltpu.VMEM(wide, BF16),
            dma((6,)), dma((steps,)), dma((steps,)), dma((steps,)), dma((steps,)),
            dma((steps,)), dma((steps,)), dma((heads // 2,)),
        ],
        compiler_params=pltpu.CompilerParams(
            collective_id=0, has_side_effects=True, vmem_limit_bytes=60 * 1024 * 1024
        ),
        cost_estimate=pl.CostEstimate(
            flops=2 * 5 * 9 * heads * half * half * HD, bytes_accessed=4 * rows * width * 2,
            transcendentals=9 * heads * half * half,
        ),
    )(
        span_table.T, queries.reshape(wide), key_rows.reshape(narrow), value_rows.reshape(narrow),
        out_grad.reshape(wide), outputs.reshape(wide), log_sum,
    )
    return dq.reshape(rows, width), dk.reshape(rows, HD), dv.reshape(rows, HD)


def solution(mesh):
    rows = P(("outer", "inner"), None)
    return jax.shard_map(
        functools.partial(per_device, mesh.shape["outer"], mesh.shape["inner"]),
        mesh=mesh,
        in_specs=(rows, rows, rows, rows, rows, P(None, ("outer", "inner")), P()),
        out_specs=(rows, rows, rows),
        check_vma=False,
    )
```

time: 58.3 us -> 26.7 us (0.46)
  matrix products: 22.5 us -> 0 us
  Pallas kernels: 0 us -> 21.9 us
  starting transfers between devices: 18.9 us -> 0 us
  waiting for transfers between devices: 8.3 us -> 0 us
  other arithmetic: 4 us -> 0 us
  local copies, waits for them, and re-layouts: 3.36 us -> 3.95 us
    dot_general x20 -> x0, matrix products: 22.5 us -> none  [the longest x4 8.14 us: block_grads(): jnp.einsum('qgd,kd->gqk', grad_block, value_block, preferred_element_type...]
    pallas_call x0 -> x1, Pallas kernels: none -> 21.9 us  [per_device(): pl.pallas_call(functools.partial(kernel, outer_count, inner_count, heads)...]
    ppermute x16 -> x0, starting transfers between devices: 18.9 us -> none  [shifted(): lax.ppermute(shard, axis, [(i, (i + by) % devices) for i in range(devices)])]
    ppermute x16 -> x0, waiting for transfers between devices: 8.3 us -> none  [shifted(): lax.ppermute(shard, axis, [(i, (i + by) % devices) for i in range(devices)])]
    unnamed x1 -> x0, other arithmetic: 1.46 us -> none
    mul x2 -> x0, other arithmetic: 0.89 us -> none  [the longest x1 0.67 us: per_device(): return (query_grad, key_total * factor, value_total)]
    add x3 -> x0, other arithmetic: 0.81 us -> none  [the longest x1 0.67 us: per_device(): value_total = value_total + carried[1]]
    unnamed x17 -> x7, local copies, waits for them, and re-layouts: 3.3 us -> 3.95 us
  transfers between devices with their start and end apart: 16 -> 0, of which waited for: 5 -> 0; matrix products, arithmetic and copies ran while one was open for 50% -> 0% of each run, Pallas kernels for 0% -> 0%
where the time goes in v1:
time: 26.7 us; the launch traced here: 26.5 us
  Pallas kernels  21.9 us (82%)
  local copies, waits for them, and re-layouts  3.95 us (15%)
  between operations  0.65 us (2%)
    pallas_call x1, Pallas kernels, per_device(): pl.pallas_call(functools.partial(kernel, outer_count, inner_count, heads)...  21.9 us
    unnamed x7, local copies, waits for them, and re-layouts  3.95 us

profile of v1, /device:TPU:0, one launch (start us, length us, event | category | flops | bytes accessed | tf_op | source)
XLA Modules:
  0.0 26.5 jit_solution(8372580803258829640)
XLA Ops:
  0.6 21.9 %shard_map.94 = (bf16[2,128,2048]{2,1,0:T(8,128)(2,1)}, f32[2,128,128]{2,1,0:T(8,128)}, f32[2,128,128]{2,1,0:T(8,128)}) custom-call(s32[2,32]{1,0:T(2,128)} %bitcast.17, bf16[2,128,2048]{2,1,0:T(8,128)(2,1)} %bitcast.12, bf16[2,128,128]{2,1,0:T(8,128)(2,1)} %bitcast.15, bf16[2,128,128]{2,1,0:T(8,128)(2,1)} %bitcast.16, bf16[2,128,2048]{2,1,0:T(8,128)(2,1)} %bitcast.13, ...), custom_call_target="tpu_custom_call" | custom-call | flops 3019898880 | bytes 4194304 | tf_op jit(solution)/shard_map/pallas_call | solution.py:222
  22.6 0.0 copy-start.1
  22.6 2.3 %copy.13 = bf16[256,2048]{1,0:T(8,128)(2,1)} copy(bf16[256,2048]{1,0:T(8,128)(2,1)} %bitcast.9) | data formatting | bytes 2097152
  24.9 0.0 copy-done.1
  24.9 0.0 copy-start
  24.9 0.7 %copy.14 = f32[256,128]{1,0:T(8,128)} copy(f32[256,128]{1,0:T(8,128)S(1)} %bitcast.11) | data formatting | bytes 262144
  25.6 0.3 %copy-done = f32[2,128,128]{2,1,0:T(8,128)S(1)} copy-done((f32[2,128,128]{2,1,0:T(8,128)S(1)}, f32[2,128,128]{2,1,0:T(8,128)}, u32[]{:S(2)}) %copy-start) | copy-done | bytes 131096
  25.9 0.7 %copy.15 = f32[256,128]{1,0:T(8,128)} copy(f32[256,128]{1,0:T(8,128)S(1)} %bitcast.10) | data formatting | bytes 262144
Async XLA Ops:
  22.6 2.4 %copy-start.1 = (f32[2,128,128]{2,1,0:T(8,128)S(1)}, f32[2,128,128]{2,1,0:T(8,128)}, u32[]{:S(2)}) copy-start(f32[2,128,128]{2,1,0:T(8,128)} %get-tuple-element.7) | copy-start | bytes 393220
  24.9 1.0 %copy-start = (f32[2,128,128]{2,1,0:T(8,128)S(1)}, f32[2,128,128]{2,1,0:T(8,128)}, u32[]{:S(2)}) copy-start(f32[2,128,128]{2,1,0:T(8,128)} %get-tuple-element.8) | copy-start | bytes 393220

commit v2 on v1

--- a/solution.py
+++ b/solution.py
@@ -30,7 +30,7 @@
     outer_count, inner_count, heads,
     span_ref, q_hbm, k_hbm, v_hbm, do_hbm, o_hbm, lse_hbm,
     dq_hbm, dk_ref, dv_ref,
-    q, do, o, own_k, own_v, lse, lse2, rdot,
+    q, do, o, q_t, do_t, own_k, own_v, lse, lse2, rdot,
     kin_a, kin_b, kin_c, vin_a, vin_b, vin_c, pin, pout, p_t, ds_t, dq_l, dq_stage,
     in_sem, ks_send, ks_recv, vs_send, vs_recv, ps_send, ps_recv, out_sem,
 ):
@@ -79,9 +79,6 @@
     def cols(h):
         return slice(h * HD, (h + 1) * HD)
 
-    def pair_rows(ref, half, p):
-        return jnp.concatenate([ref[half, :, cols(2 * p)], ref[half, :, cols(2 * p + 1)]], axis=0)
-
     def all_rows(ref, half):
         return jnp.concatenate([ref[half, :, cols(h)] for h in range(heads)], axis=0)
 
@@ -107,12 +104,17 @@
             rdot[s, 2 * p : 2 * p + 1, :] = sums[0:1, :HD]
             rdot[s, 2 * p + 1 : 2 * p + 2, :] = sums[0:1, HD:]
     loads[5].wait()
+    for s in range(2):
+        for h in range(heads):
+            q_t[s, :, cols(h)] = q[s, :, cols(h)].T
+            do_t[s, :, cols(h)] = do[s, :, cols(h)].T
 
     scale2 = factor * LOG2E
 
     def weights(keys, values, half, p, mask):
-        scores = dot_nt(keys, pair_rows(q, half, p))
-        dprobs = dot_nt(values, pair_rows(do, half, p))
+        lanes = slice(2 * p * HD, (2 * p + 2) * HD)
+        scores = dot(keys, q_t[half, :, lanes])
+        dprobs = dot(values, do_t[half, :, lanes])
         probs = jnp.exp2(scores * scale2 - pair_lanes(lse2, half, p))
         if mask is not None:
             probs = jnp.where(mask, probs, 0.0)
@@ -208,6 +210,17 @@
         p_copies[j].wait_send()
 
 
+def place(dq, dk, dv, dq_out, dk_out, dv_out, sem):
+    copies = [
+        pltpu.make_async_copy(src, dst, sem.at[n])
+        for n, (src, dst) in enumerate(((dq, dq_out), (dk, dk_out), (dv, dv_out)))
+    ]
+    for copy in copies:
+        copy.start()
+    for copy in copies:
+        copy.wait()
+
+
 def per_device(outer_count, inner_count, queries, key_rows, value_rows, out_grad, outputs, log_sum, span_table):
     heads = log_sum.shape[0]
     rows, width = queries.shape
@@ -226,10 +239,10 @@
             jax.ShapeDtypeStruct(narrow, F32),
             jax.ShapeDtypeStruct(narrow, F32),
         ),
-        in_specs=[smem] + [any_spec] * 6,
+        in_specs=[smem] + [pl.BlockSpec(memory_space=pltpu.HBM)] * 6,
         out_specs=(any_spec, vmem, vmem),
         scratch_shapes=[
-            pltpu.VMEM(wide, BF16), pltpu.VMEM(wide, BF16), pltpu.VMEM(wide, BF16),
+            *[pltpu.VMEM(wide, BF16) for _ in range(5)],
             pltpu.VMEM(narrow, BF16), pltpu.VMEM(narrow, BF16),
             pltpu.VMEM((heads, rows), F32), pltpu.VMEM((2, heads, half), F32), pltpu.VMEM((2, heads, half), F32),
             *[pltpu.VMEM(narrow, BF16) for _ in range(2 * steps)],
@@ -252,6 +265,18 @@
         span_table.T, queries.reshape(wide), key_rows.reshape(narrow), value_rows.reshape(narrow),
         out_grad.reshape(wide), outputs.reshape(wide), log_sum,
     )
+    dq, dk, dv = pl.pallas_call(
+        place,
+        out_shape=(
+            jax.ShapeDtypeStruct(wide, BF16),
+            jax.ShapeDtypeStruct(narrow, F32),
+            jax.ShapeDtypeStruct(narrow, F32),
+        ),
+        in_specs=[any_spec] * 3,
+        out_specs=[any_spec] * 3,
+        scratch_shapes=[dma((3,))],
+        compiler_params=pltpu.CompilerParams(vmem_limit_bytes=60 * 1024 * 1024),
+    )(dq, dk, dv)
     return dq.reshape(rows, width), dk.reshape(rows, HD), dv.reshape(rows, HD)
 
 

time: 26.7 us -> 63.6 us (2.38)
  Pallas kernels: 21.9 us -> 62.8 us
  local copies, waits for them, and re-layouts: 3.95 us -> 0 us
    pallas_call x0 -> x1, Pallas kernels: none -> 40.8 us  [per_device(): pl.pallas_call(place, out_shape=(jax.ShapeDtypeStruct(wide, BF16), jax.Sh...]
    unnamed x7 -> x0, local copies, waits for them, and re-layouts: 3.95 us -> none
where the time goes in v2:
time: 63.6 us; the launch traced here: 63.4 us
  Pallas kernels  62.8 us (99%)
  between operations  0.64 us (1%)
    pallas_call x1, Pallas kernels, per_device(): pl.pallas_call(place, out_shape=(jax.ShapeDtypeStruct(wide, BF16), jax.Sh...  40.8 us
    pallas_call x1, Pallas kernels, per_device(): pl.pallas_call(functools.partial(kernel, outer_count, inner_count, heads)...  21.9 us

profile of v2, /device:TPU:0, one launch (start us, length us, event | category | flops | bytes accessed | tf_op | source)
XLA Modules:
  0.0 63.4 jit_solution(1027375462871215978)
XLA Ops:
  0.6 21.9 %shard_map.94 = (bf16[2,128,2048]{2,1,0:T(8,128)(2,1)}, f32[2,128,128]{2,1,0:T(8,128)}, f32[2,128,128]{2,1,0:T(8,128)}) custom-call(s32[2,32]{1,0:T(2,128)} %bitcast.17, bf16[2,128,2048]{2,1,0:T(8,128)(2,1)} %bitcast.9, bf16[2,128,128]{2,1,0:T(8,128)(2,1)} %bitcast.15, bf16[2,128,128]{2,1,0:T(8,128)(2,1)} %bitcast.16, bf16[2,128,2048]{2,1,0:T(8,128)(2,1)} %bitcast.10, ...), custom_call_target="tpu_custom_call" | custom-call | flops 3019898880 | bytes 4194304 | tf_op jit(solution)/shard_map/pallas_call | solution.py:235
  22.6 40.8 %shard_map.95 = (bf16[2,128,2048]{2,1,0:T(8,128)(2,1)}, f32[2,128,128]{2,1,0:T(8,128)}, f32[2,128,128]{2,1,0:T(8,128)}) custom-call(bf16[2,128,2048]{2,1,0:T(8,128)(2,1)} %get-tuple-element.9.dq, f32[2,128,128]{2,1,0:T(8,128)} %get-tuple-element.10.dk, f32[2,128,128]{2,1,0:T(8,128)} %get-tuple-element.11.dv), custom_call_target="tpu_custom_call" | custom-call | tf_op jit(solution)/shard_map/pallas_call | solution.py:268

commit v3 on v1

--- a/solution.py
+++ b/solution.py
@@ -14,8 +14,7 @@
 F32 = jnp.float32
 BF16 = jnp.bfloat16
 
-STEPS = ((0, 1), (1, 0), (1, 1))
-SEND_ORDER = (1, 2, 0)
+STEPS = ((1, 0), (0, 1), (1, 1))
 
 
 def dot_nt(a, b):
@@ -65,16 +64,19 @@
     pl.semaphore_wait(barrier, 2 * len(STEPS))
 
     k_copies, v_copies = {}, {}
-    for j in SEND_ORDER:
+
+    def send_block(j, k_src, v_src, to):
         for table, src, dst, ssem, rsem in (
-            (k_copies, k_hbm, kin, ks_send, ks_recv),
-            (v_copies, v_hbm, vin, vs_send, vs_recv),
+            (k_copies, k_src, kin, ks_send, ks_recv), (v_copies, v_src, vin, vs_send, vs_recv)
         ):
             table[j] = pltpu.make_async_remote_copy(
                 src_ref=src, dst_ref=dst[j], send_sem=ssem.at[j], recv_sem=rsem.at[j],
-                device_id=ahead(STEPS[j]), device_id_type=MESH,
+                device_id=ahead(to), device_id_type=MESH,
             )
             table[j].start()
+
+    send_block(0, k_hbm, v_hbm, STEPS[0])
+    send_block(1, k_hbm, v_hbm, STEPS[1])
 
     def cols(h):
         return slice(h * HD, (h + 1) * HD)
@@ -132,6 +134,10 @@
             probs, dscores = weights(keys, values, half, p, mask)
             p_t[row * HD : (row + 1) * HD, lanes] = probs
             ds_t[row * HD : (row + 1) * HD, lanes] = dscores
+    k_copies[0].wait_recv()
+    v_copies[0].wait_recv()
+    send_block(2, kin[0], vin[0], STEPS[1])
+
     for out, lhs, rhs in ((dv_ref, p_t, do), (dk_ref, ds_t, q)):
         late = dot(lhs[HD : 3 * HD, :], all_rows(rhs, 1))
         out[0] = late[:HD] + dot(lhs[:HD, :], all_rows(rhs, 0))
@@ -152,8 +158,9 @@
         src_span = span_ref[0, src_o * inner_count + src_i]
         early = src_span < me_span
         half = jnp.where(early, 0, 1)
-        k_copies[j].wait_recv()
-        v_copies[j].wait_recv()
+        if j > 0:
+            k_copies[j].wait_recv()
+            v_copies[j].wait_recv()
         lo_k, sel_k = kin[j][0], kin[j][half]
         lo_v, sel_v = vin[j][0], vin[j][half]
         base = (3 + 2 * j) * HD
@@ -206,6 +213,24 @@
         k_copies[j].wait_send()
         v_copies[j].wait_send()
         p_copies[j].wait_send()
+
+
+def place(dq, dk, dv, dq_out, dk_out, dv_out, dq_v, dk_v, dv_v, sem_in, sem_out):
+    rows = dq.shape[1] // 2
+    pieces = [
+        tuple(ref.at[s, pl.ds(r * rows, rows), :] for ref in (dq, dq_v, dq_out))
+        for s in range(2)
+        for r in range(2)
+    ] + [(dk, dk_v, dk_out), (dv, dv_v, dv_out)]
+    loads = [pltpu.make_async_copy(src, mid, sem_in.at[n]) for n, (src, mid, _) in enumerate(pieces)]
+    stores = [pltpu.make_async_copy(mid, dst, sem_out.at[n]) for n, (_, mid, dst) in enumerate(pieces)]
+    for load in loads:
+        load.start()
+    for load, store in zip(loads, stores):
+        load.wait()
+        store.start()
+    for store in stores:
+        store.wait()
 
 
 def per_device(outer_count, inner_count, queries, key_rows, value_rows, out_grad, outputs, log_sum, span_table):
@@ -252,6 +277,20 @@
         span_table.T, queries.reshape(wide), key_rows.reshape(narrow), value_rows.reshape(narrow),
         out_grad.reshape(wide), outputs.reshape(wide), log_sum,
     )
+    dq, dk, dv = pl.pallas_call(
+        place,
+        out_shape=(
+            jax.ShapeDtypeStruct(wide, BF16),
+            jax.ShapeDtypeStruct(narrow, F32),
+            jax.ShapeDtypeStruct(narrow, F32),
+        ),
+        in_specs=[any_spec] * 3,
+        out_specs=[any_spec] * 3,
+        scratch_shapes=[
+            pltpu.VMEM(wide, BF16), pltpu.VMEM(narrow, F32), pltpu.VMEM(narrow, F32), dma((6,)), dma((6,))
+        ],
+        compiler_params=pltpu.CompilerParams(vmem_limit_bytes=60 * 1024 * 1024),
+    )(dq, dk, dv)
     return dq.reshape(rows, width), dk.reshape(rows, HD), dv.reshape(rows, HD)
 
 

time: 26.7 us -> 24 us (0.90)
  local copies, waits for them, and re-layouts: 3.95 us -> 0 us
  Pallas kernels: 21.9 us -> 23.2 us
    unnamed x7 -> x0, local copies, waits for them, and re-layouts: 3.95 us -> none
    pallas_call x0 -> x1, Pallas kernels: none -> 2.1 us  [per_device(): pl.pallas_call(place, out_shape=(jax.ShapeDtypeStruct(wide, BF16), jax.Sh...]
    pallas_call x1, Pallas kernels: 21.9 us -> 21.1 us  [per_device(): pl.pallas_call(functools.partial(kernel, outer_count, inner_count, heads)...]
where the time goes in v3:
time: 24 us; the launch traced here: 23.8 us
  Pallas kernels  23.2 us (97%)
  between operations  0.64 us (3%)
    pallas_call x1, Pallas kernels, per_device(): pl.pallas_call(functools.partial(kernel, outer_count, inner_count, heads)...  21.1 us
    pallas_call x1, Pallas kernels, per_device(): pl.pallas_call(place, out_shape=(jax.ShapeDtypeStruct(wide, BF16), jax.Sh...  2.1 us

profile of v3, /device:TPU:0, one launch (start us, length us, event | category | flops | bytes accessed | tf_op | source)
XLA Modules:
  0.0 23.8 jit_solution(2876699810038547603)
XLA Ops:
  0.6 21.1 %shard_map.94 = (bf16[2,128,2048]{2,1,0:T(8,128)(2,1)}, f32[2,128,128]{2,1,0:T(8,128)}, f32[2,128,128]{2,1,0:T(8,128)}) custom-call(s32[2,32]{1,0:T(2,128)} %bitcast.17, bf16[2,128,2048]{2,1,0:T(8,128)(2,1)} %bitcast.9, bf16[2,128,128]{2,1,0:T(8,128)(2,1)} %bitcast.15, bf16[2,128,128]{2,1,0:T(8,128)(2,1)} %bitcast.16, bf16[2,128,2048]{2,1,0:T(8,128)(2,1)} %bitcast.10, ...), custom_call_target="tpu_custom_call" | custom-call | flops 3019898880 | bytes 4194304 | tf_op jit(solution)/shard_map/pallas_call | solution.py:247
  21.7 2.1 %shard_map.95 = (bf16[2,128,2048]{2,1,0:T(8,128)(2,1)}, f32[2,128,128]{2,1,0:T(8,128)}, f32[2,128,128]{2,1,0:T(8,128)}) custom-call(bf16[2,128,2048]{2,1,0:T(8,128)(2,1)} %get-tuple-element.9.dq, f32[2,128,128]{2,1,0:T(8,128)} %get-tuple-element.10.dk, f32[2,128,128]{2,1,0:T(8,128)} %get-tuple-element.11.dv), custom_call_target="tpu_custom_call" | custom-call | tf_op jit(solution)/shard_map/pallas_call | solution.py:280

commit v4 on v3

--- a/solution.py
+++ b/solution.py
@@ -28,9 +28,9 @@
 def kernel(
     outer_count, inner_count, heads,
     span_ref, q_hbm, k_hbm, v_hbm, do_hbm, o_hbm, lse_hbm,
-    dq_hbm, dk_ref, dv_ref,
+    dq_hbm, own_hbm, pin,
     q, do, o, own_k, own_v, lse, lse2, rdot,
-    kin_a, kin_b, kin_c, vin_a, vin_b, vin_c, pin, pout, p_t, ds_t, dq_l, dq_stage,
+    kin_a, kin_b, kin_c, vin_a, vin_b, vin_c, pout, own, p_own, p_t, ds_t, dq_l, dq_stage,
     in_sem, ks_send, ks_recv, vs_send, vs_recv, ps_send, ps_recv, out_sem,
 ):
     me_o = lax.axis_index("outer")
@@ -65,18 +65,17 @@
 
     k_copies, v_copies = {}, {}
 
-    def send_block(j, k_src, v_src, to):
-        for table, src, dst, ssem, rsem in (
-            (k_copies, k_src, kin, ks_send, ks_recv), (v_copies, v_src, vin, vs_send, vs_recv)
-        ):
-            table[j] = pltpu.make_async_remote_copy(
-                src_ref=src, dst_ref=dst[j], send_sem=ssem.at[j], recv_sem=rsem.at[j],
-                device_id=ahead(to), device_id_type=MESH,
-            )
-            table[j].start()
-
-    send_block(0, k_hbm, v_hbm, STEPS[0])
-    send_block(1, k_hbm, v_hbm, STEPS[1])
+    def send(j, table, src, dst, ssem, rsem):
+        to = STEPS[min(j, 1)]
+        table[j] = pltpu.make_async_remote_copy(
+            src_ref=src, dst_ref=dst[j], send_sem=ssem.at[j], recv_sem=rsem.at[j],
+            device_id=ahead(to), device_id_type=MESH,
+        )
+        table[j].start()
+
+    for j in range(2):
+        send(j, k_copies, k_hbm, kin, ks_send, ks_recv)
+        send(j, v_copies, v_hbm, vin, vs_send, vs_recv)
 
     def cols(h):
         return slice(h * HD, (h + 1) * HD)
@@ -132,16 +131,14 @@
             (0, lo_k, lo_v, 0, triangle), (1, lo_k, lo_v, 1, None), (2, hi_k, hi_v, 1, triangle)
         ):
             probs, dscores = weights(keys, values, half, p, mask)
-            p_t[row * HD : (row + 1) * HD, lanes] = probs
+            p_own[row * HD : (row + 1) * HD, lanes] = probs
             ds_t[row * HD : (row + 1) * HD, lanes] = dscores
-    k_copies[0].wait_recv()
-    v_copies[0].wait_recv()
-    send_block(2, kin[0], vin[0], STEPS[1])
-
-    for out, lhs, rhs in ((dv_ref, p_t, do), (dk_ref, ds_t, q)):
-        late = dot(lhs[HD : 3 * HD, :], all_rows(rhs, 1))
-        out[0] = late[:HD] + dot(lhs[:HD, :], all_rows(rhs, 0))
-        out[1] = late[HD:]
+        if p == pairs // 4:
+            k_copies[0].wait_recv()
+            send(2, k_copies, kin[0], kin, ks_send, ks_recv)
+        if p == pairs // 2:
+            v_copies[0].wait_recv()
+            send(2, v_copies, vin[0], vin, vs_send, vs_recv)
 
     zero = jnp.zeros((HD, HD), BF16)
     dq_l[0:HD, 0:HD] = zero
@@ -171,22 +168,31 @@
                 p_t[row * HD : (row + 1) * HD, lanes] = probs
                 ds_t[base + row * HD : base + (row + 1) * HD, lanes] = dscores
         is_early = jnp.full((HD, HD), src_span, jnp.int32) < me_span
-        for n, (lhs, at, rhs) in enumerate(((ds_t, base, q), (p_t, 0, do))):
+        for n, lhs, at, rhs in ((1, p_t, 0, do), (0, ds_t, base, q)):
             on_lo = dot(lhs[at : at + HD, :], all_rows(rhs, 1))
             on_sel = dot(lhs[at + HD : at + 2 * HD, :], all_rows(rhs, half))
             pout[j, 2 * n] = (on_lo + jnp.where(is_early, on_sel, 0.0)).astype(BF16)
             pout[j, 2 * n + 1] = jnp.where(is_early, 0.0, on_sel).astype(BF16)
-        copy = pltpu.make_async_remote_copy(
-            src_ref=pout.at[j], dst_ref=pin.at[j], send_sem=ps_send.at[j], recv_sem=ps_recv.at[j],
-            device_id=behind(step), device_id_type=MESH,
-        )
-        copy.start()
-        p_copies.append(copy)
+            part = pl.ds(2 * n, 2)
+            copy = pltpu.make_async_remote_copy(
+                src_ref=pout.at[j, part], dst_ref=pin.at[j, part],
+                send_sem=ps_send.at[2 * j + n], recv_sem=ps_recv.at[2 * j + n],
+                device_id=behind(step), device_id_type=MESH,
+            )
+            copy.start()
+            p_copies.append(copy)
         sel_t = sel_k.astype(F32).T
         dq_l[0:HD, base : base + HD] = lo_k.T
         dq_l[0:HD, base + HD : base + 2 * HD] = jnp.where(is_early, 0.0, sel_t).astype(BF16)
         dq_l[HD:, base : base + HD] = zero
         dq_l[HD:, base + HD : base + 2 * HD] = jnp.where(is_early, sel_t, 0.0).astype(BF16)
+
+    for n, lhs, rhs in ((0, ds_t, q), (1, p_own, do)):
+        late = dot(lhs[HD : 3 * HD, :], all_rows(rhs, 1))
+        own[n, 0] = late[:HD] + dot(lhs[:HD, :], all_rows(rhs, 0))
+        own[n, 1] = late[HD:]
+    own_store = pltpu.make_async_copy(own, own_hbm, out_sem.at[pairs])
+    own_store.start()
 
     stores = []
     for p in range(pairs):
@@ -202,33 +208,44 @@
         store.start()
         stores.append(store)
 
-    for j in range(len(STEPS)):
-        p_copies[j].wait_recv()
-    for s in range(2):
-        dk_ref[s] = (dk_ref[s] + sum(pin[j, s].astype(F32) for j in range(len(STEPS)))) * factor
-        dv_ref[s] = dv_ref[s] + sum(pin[j, 2 + s].astype(F32) for j in range(len(STEPS)))
+    own_store.wait()
     for store in stores:
         store.wait()
+    for copy in p_copies:
+        copy.wait_recv()
     for j in range(len(STEPS)):
         k_copies[j].wait_send()
         v_copies[j].wait_send()
-        p_copies[j].wait_send()
-
-
-def place(dq, dk, dv, dq_out, dk_out, dv_out, dq_v, dk_v, dv_v, sem_in, sem_out):
+    for copy in p_copies:
+        copy.wait_send()
+
+
+def place(dq, own, parts, dq_out, dk_out, dv_out, dq_v, own_v, parts_v, dk_v, dv_v, sem_in, sem_out):
     rows = dq.shape[1] // 2
     pieces = [
         tuple(ref.at[s, pl.ds(r * rows, rows), :] for ref in (dq, dq_v, dq_out))
         for s in range(2)
         for r in range(2)
-    ] + [(dk, dk_v, dk_out), (dv, dv_v, dv_out)]
-    loads = [pltpu.make_async_copy(src, mid, sem_in.at[n]) for n, (src, mid, _) in enumerate(pieces)]
-    stores = [pltpu.make_async_copy(mid, dst, sem_out.at[n]) for n, (_, mid, dst) in enumerate(pieces)]
+    ]
+    count = len(pieces)
+    moves = [(own, own_v), (parts, parts_v)] + [piece[:2] for piece in pieces]
+    loads = [pltpu.make_async_copy(src, mid, sem_in.at[n]) for n, (src, mid) in enumerate(moves)]
+    moves = [piece[1:] for piece in pieces] + [(dk_v, dk_out), (dv_v, dv_out)]
+    stores = [pltpu.make_async_copy(mid, dst, sem_out.at[n]) for n, (mid, dst) in enumerate(moves)]
     for load in loads:
         load.start()
-    for load, store in zip(loads, stores):
-        load.wait()
-        store.start()
+    loads[0].wait()
+    loads[1].wait()
+    for n, (out, scale) in enumerate(((dk_v, 1.0 / math.sqrt(HD)), (dv_v, 1.0))):
+        for s in range(2):
+            total = own_v[n, s]
+            for j in range(parts.shape[0]):
+                total = total + parts_v[j, 2 * n + s].astype(F32)
+            out[s] = total * scale
+        stores[count + n].start()
+    for n in range(count):
+        loads[2 + n].wait()
+        stores[n].start()
     for store in stores:
         store.wait()
 
@@ -239,32 +256,31 @@
     half = rows // 2
     steps = len(STEPS)
     any_spec = pl.BlockSpec(memory_space=pl.ANY)
-    vmem = pl.BlockSpec(memory_space=pltpu.VMEM)
     smem = pl.BlockSpec(memory_space=pltpu.SMEM)
     wide = (2, half, width)
     narrow = (2, half, HD)
     dma = pltpu.SemaphoreType.DMA
-    dq, dk, dv = pl.pallas_call(
+    dq, own, parts = pl.pallas_call(
         functools.partial(kernel, outer_count, inner_count, heads),
         out_shape=(
             jax.ShapeDtypeStruct(wide, BF16),
-            jax.ShapeDtypeStruct(narrow, F32),
-            jax.ShapeDtypeStruct(narrow, F32),
+            jax.ShapeDtypeStruct((2,) + narrow, F32),
+            jax.ShapeDtypeStruct((steps, 4, half, HD), BF16),
         ),
         in_specs=[smem] + [any_spec] * 6,
-        out_specs=(any_spec, vmem, vmem),
+        out_specs=(any_spec,) * 3,
         scratch_shapes=[
             pltpu.VMEM(wide, BF16), pltpu.VMEM(wide, BF16), pltpu.VMEM(wide, BF16),
             pltpu.VMEM(narrow, BF16), pltpu.VMEM(narrow, BF16),
             pltpu.VMEM((heads, rows), F32), pltpu.VMEM((2, heads, half), F32), pltpu.VMEM((2, heads, half), F32),
             *[pltpu.VMEM(narrow, BF16) for _ in range(2 * steps)],
-            pltpu.VMEM((steps, 4, half, HD), BF16), pltpu.VMEM((steps, 4, half, HD), BF16),
-            pltpu.VMEM((3 * half, width), BF16),
+            pltpu.VMEM((steps, 4, half, HD), BF16), pltpu.VMEM((2,) + narrow, F32),
+            pltpu.VMEM((3 * half, width), BF16), pltpu.VMEM((2 * half, width), BF16),
             pltpu.VMEM(((3 + 2 * steps) * half, width), BF16),
             pltpu.VMEM((2 * HD, (3 + 2 * steps) * half), BF16),
             pltpu.VMEM(wide, BF16),
             dma((6,)), dma((steps,)), dma((steps,)), dma((steps,)), dma((steps,)),
-            dma((steps,)), dma((steps,)), dma((heads // 2,)),
+            dma((2 * steps,)), dma((2 * steps,)), dma((heads // 2 + 1,)),
         ],
         compiler_params=pltpu.CompilerParams(
             collective_id=0, has_side_effects=True, vmem_limit_bytes=60 * 1024 * 1024
@@ -287,10 +303,11 @@
         in_specs=[any_spec] * 3,
         out_specs=[any_spec] * 3,
         scratch_shapes=[
-            pltpu.VMEM(wide, BF16), pltpu.VMEM(narrow, F32), pltpu.VMEM(narrow, F32), dma((6,)), dma((6,))
+            pltpu.VMEM(wide, BF16), pltpu.VMEM((2,) + narrow, F32), pltpu.VMEM((steps, 4, half, HD), BF16),
+            pltpu.VMEM(narrow, F32), pltpu.VMEM(narrow, F32), dma((6,)), dma((6,)),
         ],
         compiler_params=pltpu.CompilerParams(vmem_limit_bytes=60 * 1024 * 1024),
-    )(dq, dk, dv)
+    )(dq, own, parts)
     return dq.reshape(rows, width), dk.reshape(rows, HD), dv.reshape(rows, HD)
 
 

time: 24 us -> 23 us (0.958)
  Pallas kernels: 23.2 us -> 22.2 us
    pallas_call x1, Pallas kernels: 21.1 us -> 19.9 us  [per_device(): pl.pallas_call(functools.partial(kernel, outer_count, inner_count, heads)...]
where the time goes in v4:
time: 23 us; the launch traced here: 22.8 us
  Pallas kernels  22.2 us (97%)
  between operations  0.64 us (3%)
    pallas_call x1, Pallas kernels, per_device(): pl.pallas_call(functools.partial(kernel, outer_count, inner_count, heads)...  19.9 us
    pallas_call x1, Pallas kernels, per_device(): pl.pallas_call(place, out_shape=(jax.ShapeDtypeStruct(wide, BF16), jax.Sh...  2.26 us

profile of v4, /device:TPU:0, one launch (start us, length us, event | category | flops | bytes accessed | tf_op | source)
XLA Modules:
  0.0 22.8 jit_solution(5724183715593186309)
XLA Ops:
  0.6 19.9 %shard_map.94 = (bf16[2,128,2048]{2,1,0:T(8,128)(2,1)}, f32[2,2,128,128]{3,2,1,0:T(8,128)}, bf16[3,4,128,128]{3,2,1,0:T(8,128)(2,1)}) custom-call(s32[2,32]{1,0:T(2,128)} %bitcast.17, bf16[2,128,2048]{2,1,0:T(8,128)(2,1)} %bitcast.9, bf16[2,128,128]{2,1,0:T(8,128)(2,1)} %bitcast.15, bf16[2,128,128]{2,1,0:T(8,128)(2,1)} %bitcast.16, ...), custom_call_target="tpu_custom_call" | custom-call | flops 3019898880 | bytes 4194304 | tf_op jit(solution)/shard_map/pallas_call | solution.py:263
  20.5 2.3 %shard_map.95 = (bf16[2,128,2048]{2,1,0:T(8,128)(2,1)}, f32[2,128,128]{2,1,0:T(8,128)}, f32[2,128,128]{2,1,0:T(8,128)}) custom-call(bf16[2,128,2048]{2,1,0:T(8,128)(2,1)} %get-tuple-element.9.dq, f32[2,2,128,128]{3,2,1,0:T(8,128)} %get-tuple-element.10.own, bf16[3,4,128,128]{3,2,1,0:T(8,128)(2,1)} %get-tuple-element.11.parts), custom_call_target="tpu_custom_call" | custom-call | tf_op jit(solution)/shard_map/pallas_call | solution.py:296

commit v5 on v4

--- a/solution.py
+++ b/solution.py
@@ -71,24 +71,42 @@
             src_ref=src, dst_ref=dst[j], send_sem=ssem.at[j], recv_sem=rsem.at[j],
             device_id=ahead(to), device_id_type=MESH,
         )
-        table[j].start()
-
+
+    for j in range(3):
+        send(j, k_copies, kin[0] if j == 2 else k_hbm, kin, ks_send, ks_recv)
+        send(j, v_copies, vin[0] if j == 2 else v_hbm, vin, vs_send, vs_recv)
     for j in range(2):
-        send(j, k_copies, k_hbm, kin, ks_send, ks_recv)
-        send(j, v_copies, v_hbm, vin, vs_send, vs_recv)
+        k_copies[j].start()
+        v_copies[j].start()
 
     def cols(h):
         return slice(h * HD, (h + 1) * HD)
 
+    def head_lanes(h):
+        return pl.ds(pl.multiple_of(h * HD, HD), HD)
+
+    def two_lanes(p):
+        return pl.ds(pl.multiple_of(p * 2 * HD, 2 * HD), 2 * HD)
+
     def pair_rows(ref, half, p):
-        return jnp.concatenate([ref[half, :, cols(2 * p)], ref[half, :, cols(2 * p + 1)]], axis=0)
+        return jnp.concatenate(
+            [ref[half, :, head_lanes(2 * p)], ref[half, :, head_lanes(2 * p + 1)]], axis=0
+        )
+
+    def over_pairs(body):
+        def turn(n, carry):
+            body(2 * n)
+            body(2 * n + 1)
+            return carry
+
+        lax.fori_loop(0, pairs // 2, turn, 0)
 
     def all_rows(ref, half):
         return jnp.concatenate([ref[half, :, cols(h)] for h in range(heads)], axis=0)
 
     def pair_lanes(ref, half, p):
         return jnp.concatenate(
-            [ref[half, 2 * p : 2 * p + 1, :], ref[half, 2 * p + 1 : 2 * p + 2, :]], axis=1
+            [ref[half, pl.ds(2 * p, 1), :], ref[half, pl.ds(2 * p + 1, 1), :]], axis=1
         )
 
     for load in loads[:5]:
@@ -96,17 +114,20 @@
     for s in range(2):
         lse2[s] = lse[:, s * HD : (s + 1) * HD] * LOG2E
     ones = jnp.ones((16, 2 * HD), BF16)
-    for s in range(2):
-        for p in range(pairs):
+
+    def row_dots(p):
+        for s in range(2):
             terms = []
             for h in (2 * p, 2 * p + 1):
-                prod = do[s, :, cols(h)].astype(F32) * o[s, :, cols(h)].astype(F32)
+                prod = do[s, :, head_lanes(h)].astype(F32) * o[s, :, head_lanes(h)].astype(F32)
                 high = prod.astype(BF16)
                 low = (prod - high.astype(F32)).astype(BF16)
                 terms.append(jnp.concatenate([high, low], axis=1))
             sums = dot_nt(ones, jnp.concatenate(terms, axis=0))
-            rdot[s, 2 * p : 2 * p + 1, :] = sums[0:1, :HD]
-            rdot[s, 2 * p + 1 : 2 * p + 2, :] = sums[0:1, HD:]
+            rdot[s, pl.ds(2 * p, 1), :] = sums[0:1, :HD]
+            rdot[s, pl.ds(2 * p + 1, 1), :] = sums[0:1, HD:]
+
+    over_pairs(row_dots)
     loads[5].wait()
 
     scale2 = factor * LOG2E
@@ -125,20 +146,32 @@
     triangle = k_rows <= q_lanes
     lo_k, hi_k = own_k[0], own_k[1]
     lo_v, hi_v = own_v[0], own_v[1]
-    for p in range(pairs):
-        lanes = slice(2 * p * HD, (2 * p + 2) * HD)
+
+    def own_pair(p):
+        lanes = two_lanes(p)
         for row, keys, values, half, mask in (
             (0, lo_k, lo_v, 0, triangle), (1, lo_k, lo_v, 1, None), (2, hi_k, hi_v, 1, triangle)
         ):
             probs, dscores = weights(keys, values, half, p, mask)
             p_own[row * HD : (row + 1) * HD, lanes] = probs
             ds_t[row * HD : (row + 1) * HD, lanes] = dscores
-        if p == pairs // 4:
+
+    def own_turn(n, carry):
+        @pl.when(n == 1)
+        def _():
             k_copies[0].wait_recv()
-            send(2, k_copies, kin[0], kin, ks_send, ks_recv)
-        if p == pairs // 2:
+            k_copies[2].start()
+
+        @pl.when(n == 2)
+        def _():
             v_copies[0].wait_recv()
-            send(2, v_copies, vin[0], vin, vs_send, vs_recv)
+            v_copies[2].start()
+
+        own_pair(2 * n)
+        own_pair(2 * n + 1)
+        return carry
+
+    lax.fori_loop(0, pairs // 2, own_turn, 0)
 
     zero = jnp.zeros((HD, HD), BF16)
     dq_l[0:HD, 0:HD] = zero
@@ -161,12 +194,15 @@
         lo_k, sel_k = kin[j][0], kin[j][half]
         lo_v, sel_v = vin[j][0], vin[j][half]
         base = (3 + 2 * j) * HD
-        for p in range(pairs):
-            lanes = slice(2 * p * HD, (2 * p + 2) * HD)
+
+        def other_pair(p):
+            lanes = two_lanes(p)
             for row, keys, values, side in ((0, lo_k, lo_v, 1), (1, sel_k, sel_v, half)):
                 probs, dscores = weights(keys, values, side, p, None)
                 p_t[row * HD : (row + 1) * HD, lanes] = probs
                 ds_t[base + row * HD : base + (row + 1) * HD, lanes] = dscores
+
+        over_pairs(other_pair)
         is_early = jnp.full((HD, HD), src_span, jnp.int32) < me_span
         for n, lhs, at, rhs in ((1, p_t, 0, do), (0, ds_t, base, q)):
             on_lo = dot(lhs[at : at + HD, :], all_rows(rhs, 1))
@@ -194,20 +230,21 @@
     own_store = pltpu.make_async_copy(own, own_hbm, out_sem.at[pairs])
     own_store.start()
 
-    stores = []
-    for p in range(pairs):
-        lanes = slice(2 * p * HD, (2 * p + 2) * HD)
-        grads = dot(dq_l[...], ds_t[:, lanes]) * factor
+    def query_store(p):
+        return pltpu.make_async_copy(
+            dq_stage.at[:, :, two_lanes(p)], dq_hbm.at[:, :, two_lanes(p)], out_sem.at[p]
+        )
+
+    def query_pair(p):
+        grads = dot(dq_l[...], ds_t[:, two_lanes(p)]) * factor
         for s in range(2):
             for n in range(2):
                 tile = grads[(1 - s) * HD : (2 - s) * HD, n * HD : (n + 1) * HD]
-                dq_stage[s, :, cols(2 * p + n)] = tile.T.astype(BF16)
-        store = pltpu.make_async_copy(
-            dq_stage.at[:, :, lanes], dq_hbm.at[:, :, lanes], out_sem.at[p]
-        )
-        store.start()
-        stores.append(store)
-
+                dq_stage[s, :, head_lanes(2 * p + n)] = tile.T.astype(BF16)
+        query_store(p).start()
+
+    over_pairs(query_pair)
+    stores = [query_store(p) for p in range(pairs)]
     own_store.wait()
     for store in stores:
         store.wait()

time: 23 us -> 26 us (1.13)
  Pallas kernels: 22.2 us -> 25.2 us
    pallas_call x1, Pallas kernels: 19.9 us -> 23 us  [per_device(): pl.pallas_call(functools.partial(kernel, outer_count, inner_count, heads)...]
where the time goes in v5:
time: 26 us; the launch traced here: 25.9 us
  Pallas kernels  25.2 us (97%)
  between operations  0.64 us (2%)
    pallas_call x1, Pallas kernels, per_device(): pl.pallas_call(functools.partial(kernel, outer_count, inner_count, heads)...  23 us
    pallas_call x1, Pallas kernels, per_device(): pl.pallas_call(place, out_shape=(jax.ShapeDtypeStruct(wide, BF16), jax.Sh...  2.26 us

profile of v5, /device:TPU:0, one launch (start us, length us, event | category | flops | bytes accessed | tf_op | source)
XLA Modules:
  0.0 25.9 jit_solution(9794095526351055259)
XLA Ops:
  0.6 23.0 %shard_map.94 = (bf16[2,128,2048]{2,1,0:T(8,128)(2,1)}, f32[2,2,128,128]{3,2,1,0:T(8,128)}, bf16[3,4,128,128]{3,2,1,0:T(8,128)(2,1)}) custom-call(s32[2,32]{1,0:T(2,128)} %bitcast.17, bf16[2,128,2048]{2,1,0:T(8,128)(2,1)} %bitcast.9, bf16[2,128,128]{2,1,0:T(8,128)(2,1)} %bitcast.15, bf16[2,128,128]{2,1,0:T(8,128)(2,1)} %bitcast.16, ...), custom_call_target="tpu_custom_call" | custom-call | flops 3019898880 | bytes 4194304 | tf_op jit(solution)/shard_map/pallas_call | solution.py:300
  23.6 2.3 %shard_map.95 = (bf16[2,128,2048]{2,1,0:T(8,128)(2,1)}, f32[2,128,128]{2,1,0:T(8,128)}, f32[2,128,128]{2,1,0:T(8,128)}) custom-call(bf16[2,128,2048]{2,1,0:T(8,128)(2,1)} %get-tuple-element.9.dq, f32[2,2,128,128]{3,2,1,0:T(8,128)} %get-tuple-element.10.own, bf16[3,4,128,128]{3,2,1,0:T(8,128)(2,1)} %get-tuple-element.11.parts), custom_call_target="tpu_custom_call" | custom-call | tf_op jit(solution)/shard_map/pallas_call | solution.py:333

commit v6 on v4

--- a/solution.py
+++ b/solution.py
@@ -150,7 +150,8 @@
 
     me_span = span_ref[0, me_o * inner_count + me_i]
     p_copies = []
-    for j, step in enumerate(STEPS):
+    for j in (0, 2, 1):
+        step = STEPS[j]
         src_o, src_i = behind(step)
         src_span = span_ref[0, src_o * inner_count + src_i]
         early = src_span < me_span

time: 23 us -> 23.5 us (1.022)
  Pallas kernels: 22.2 us -> 22.7 us
    pallas_call x1, Pallas kernels: 19.9 us -> 20.4 us  [per_device(): pl.pallas_call(functools.partial(kernel, outer_count, inner_count, heads)...]
where the time goes in v6:
time: 23.5 us; the launch traced here: 23.3 us
  Pallas kernels  22.7 us (97%)
  between operations  0.64 us (3%)
    pallas_call x1, Pallas kernels, per_device(): pl.pallas_call(functools.partial(kernel, outer_count, inner_count, heads)...  20.4 us
    pallas_call x1, Pallas kernels, per_device(): pl.pallas_call(place, out_shape=(jax.ShapeDtypeStruct(wide, BF16), jax.Sh...  2.26 us

profile of v6, /device:TPU:0, one launch (start us, length us, event | category | flops | bytes accessed | tf_op | source)
XLA Modules:
  0.0 23.3 jit_solution(997741382648533524)
XLA Ops:
  0.6 20.4 %shard_map.94 = (bf16[2,128,2048]{2,1,0:T(8,128)(2,1)}, f32[2,2,128,128]{3,2,1,0:T(8,128)}, bf16[3,4,128,128]{3,2,1,0:T(8,128)(2,1)}) custom-call(s32[2,32]{1,0:T(2,128)} %bitcast.17, bf16[2,128,2048]{2,1,0:T(8,128)(2,1)} %bitcast.9, bf16[2,128,128]{2,1,0:T(8,128)(2,1)} %bitcast.15, bf16[2,128,128]{2,1,0:T(8,128)(2,1)} %bitcast.16, ...), custom_call_target="tpu_custom_call" | custom-call | flops 3019898880 | bytes 4194304 | tf_op jit(solution)/shard_map/pallas_call | solution.py:264
  21.1 2.3 %shard_map.95 = (bf16[2,128,2048]{2,1,0:T(8,128)(2,1)}, f32[2,128,128]{2,1,0:T(8,128)}, f32[2,128,128]{2,1,0:T(8,128)}) custom-call(bf16[2,128,2048]{2,1,0:T(8,128)(2,1)} %get-tuple-element.9.dq, f32[2,2,128,128]{3,2,1,0:T(8,128)} %get-tuple-element.10.own, bf16[3,4,128,128]{3,2,1,0:T(8,128)(2,1)} %get-tuple-element.11.parts), custom_call_target="tpu_custom_call" | custom-call | tf_op jit(solution)/shard_map/pallas_call | solution.py:297
